TPU v7x, 32 devices: a whole 2x2x4 slice. The times are simulated.
32 devices in a mesh: dp: 4 (over y, x), tm: 4 (over z), height: 2 (over core).
Axes of the slice: x: 2, y: 2, z: 4, core: 2. Of those that a mesh axis runs over, the one named last changes fastest.
Arguments:
- video: bfloat16 [4, 8, 8, 64, 256], P('dp', 'tm', 'height'), may hold values from -6 to 6
- lengths: int32 [4], P('dp'), may hold values from 1 to 8
- enc_weight: bfloat16 [3, 3, 3, 256, 256], replicated, may hold values from -0.078125 to 0.078125
- dec_weight: bfloat16 [3, 3, 3, 256, 256], replicated, may hold values from -0.078125 to 0.078125
- cotangent: bfloat16 [4, 8, 8, 64, 256], P('dp', 'tm', 'height'), may hold values from -6 to 6
Outputs:
- output: bfloat16 [4, 8, 8, 64, 256], P('dp', 'tm', 'height')
- enc_grad: float32 [3, 3, 3, 256, 256], replicated
- dec_grad: float32 [3, 3, 3, 256, 256], replicated
All inputs are finite; a program needn't handle non-finite values.
Results may differ from a plain program's by a relative error of at most 0.0045.
Values may be sent and summed in bfloat16 or wider, within the bound.
A program may use at most 128 MiB of HBM per device.

v0:
```python
import jax
import jax.numpy as jnp
from jax import lax
from jax.experimental import pallas as pl
from jax.experimental.pallas import tpu as pltpu
from jax.sharding import PartitionSpec as P

MESH = pl.DeviceIdType.MESH
LAG = 1


def extended(shard, sides, width):
    for axis, dim in sides:
        devices, length = (lax.axis_size(axis), shard.shape[dim])
        up = [(i, (i + 1) % devices) for i in range(devices - 1)]
        down = [(j, i) for i, j in up]
        last = lax.slice_in_dim(shard, length - width, length, axis=dim)
        leading = lax.slice_in_dim(shard, 0, width, axis=dim)
        before = lax.ppermute(last, axis, up)
        after = lax.ppermute(leading, axis, down)
        shard = jnp.concatenate([before, shard, after], axis=dim)
    return shard


def from_behind(block, axis, distance):
    devices = range(lax.axis_size(axis))
    route = [(i - distance, i) for i in devices if i - distance in devices]
    return lax.ppermute(block, axis, route)


def apply_taps(ext, weight, transposed=False):
    count, frame_pad, row_pad, wide, chans = ext.shape
    frames = frame_pad - 2
    rows = row_pad - 2
    outs = weight.shape[2] if transposed else weight.shape[-1]
    padded = jnp.pad(ext, ((0, 0), (0, 0), (0, 0), (1, 1), (0, 0)))
    stacked = jnp.concatenate([padded[:, :, :, e : e + wide, :] for e in range(3)], axis=-1)
    total = jnp.zeros((count * frames * rows * wide, outs), jnp.float32)
    for a in range(3):
        for b in range(3):
            slab = stacked[:, a : a + frames, b : b + rows].reshape(-1, 3 * chans)
            if transposed:
                total = total + lax.dot_general(
                    slab, weight[a, b], (((1,), (1,)), ((), ())), preferred_element_type=jnp.float32
                )
                continue
            total = total + jnp.dot(
                slab, weight[a, b].reshape(3 * chans, outs), preferred_element_type=jnp.float32
            )
    return total.reshape(count, frames, rows, wide, outs)


def tap_grads(ext, cot):
    count, frame_pad, row_pad, wide, chans = ext.shape
    frames = frame_pad - 2
    rows = row_pad - 2
    outs = cot.shape[-1]
    padded = jnp.pad(ext, ((0, 0), (0, 0), (0, 0), (1, 1), (0, 0)))
    stacked = jnp.concatenate([padded[:, :, :, e : e + wide, :] for e in range(3)], axis=-1)
    flat = cot.reshape(-1, outs)
    result = []
    for a in range(3):
        for b in range(3):
            slab = stacked[:, a : a + frames, b : b + rows].reshape(-1, 3 * chans)
            result.append(
                lax.dot_general(
                    slab, flat, (((0,), (0,)), ((), ())), preferred_element_type=jnp.float32
                )
            )
    return jnp.stack(result).reshape(3, 3, 3, chans, outs)


def dsilu(value):
    sig = jax.nn.sigmoid(value)
    return sig * (1.0 + value * (1.0 - sig))


def row_edges(block):
    return extended(block, (("height", 2),), 1)


def with_earlier(block):
    before = from_behind(block, "tm", 1)
    return row_edges(jnp.concatenate([before, block], axis=1))


def with_later(block):
    after = from_behind(block, "tm", -1)
    return row_edges(jnp.concatenate([block, after], axis=1))


def index_bits(axis):
    size = lax.axis_size(axis)
    bits = []
    step = 1
    while step < size:
        bits.append((axis, step))
        step *= 2
    return bits


def swap(block, axis, step):
    return lax.ppermute(block, axis, [(i, i ^ step) for i in range(lax.axis_size(axis))])


def sum_part(part, order):
    trail = []
    for dim, (axis, step) in order:
        upper = lax.rem(lax.axis_index(axis) // step, 2) == 1
        low, high = jnp.split(part, 2, axis=dim)
        keep, give = jnp.where(upper, high, low), jnp.where(upper, low, high)
        got = swap(give.astype(jnp.bfloat16), axis, step)
        part = keep + got.astype(jnp.float32)
        trail.append((dim, axis, step, upper))
    part = part.astype(jnp.bfloat16)
    for dim, axis, step, upper in trail[::-1]:
        got = swap(part, axis, step)
        part = jnp.concatenate([jnp.where(upper, got, part), jnp.where(upper, part, got)], axis=dim)
    return part.astype(jnp.float32)


def sum_all(grad):
    height, dp, tm = index_bits("height"), index_bits("dp"), index_bits("tm")
    rest = height[1:]
    flat = grad.reshape(27, -1, grad.shape[-1])
    sums = []
    at = 0
    for count, order in ((10, dp + tm + rest), (10, dp[::-1] + tm + rest), (7, tm + dp + rest)):
        part = flat[at : at + count]
        at += count
        sums.append(sum_part(part, [(2, height[0])] + [(1, bit) for bit in order]))
    return jnp.concatenate(sums, axis=0).reshape(grad.shape)

STEPS = 9
F32 = jnp.float32
BF16 = jnp.bfloat16


def step_kernel(
    lengths, video, cot, enc_hbm, dec_hbm, output, out,
    wenc, wdec, xe, ge, he, de, xp, gp, hp, dp, ht, ds, ys, slope,
    yb, keep, give, r1, zb, rz, wsem, hs, hr, ssem, rsem,
):
    d, t, h = lax.axis_index("dp"), lax.axis_index("tm"), lax.axis_index("height")
    frames, tall, wide, chans = video.shape[1:]
    last = lax.axis_size("tm") - 1
    xbit, ybit = d % 2, d // 2
    core = (d, t, 1 - h)
    xdev = (d + 1 - 2 * xbit, t, h)
    ydev = (d + 2 - 4 * ybit, t, h)
    later = (d, lax.rem(t + 1, last + 1), h)
    earlier = (d, lax.rem(t + last, last + 1), h)
    spots = frames * tall * wide
    base = tall * h

    w_enc = pltpu.make_async_copy(enc_hbm, wenc, wsem.at[0])
    w_dec = pltpu.make_async_copy(dec_hbm, wdec, wsem.at[1])
    w_enc.start()
    w_dec.start()

    barrier = pltpu.get_barrier_semaphore()
    partners = [core, xdev, ydev] + [(d, lax.rem(t + k, last + 1), h) for k in range(1, 4)]
    for partner in partners:
        pl.semaphore_signal(barrier, inc=1, device_id=partner, device_id_type=MESH)

    rows = pl.ds(1 + base, tall)
    own_rows = pl.ds(base, tall)

    def half(first):
        return pl.ds(pl.multiple_of(128 * first, 128), 128)

    for f in range(frames):
        live = t * frames + f < lengths[0]
        xe[2 + f, rows] = jnp.where(live, video[0, f], jnp.zeros_like(video[0, f]))
        ge[f, rows] = jnp.where(live, cot[0, f], jnp.zeros_like(cot[0, f]))
    for ref in (xe, ge, he, xp, gp):
        for edge in (0, 9):
            ref[:, edge] = jnp.zeros((4,) + ref.shape[2:], BF16)

    @pl.when(t == 0)
    def _():
        for ref in (xe, he, xp):
            ref[0:2] = jnp.zeros((2,) + ref.shape[1:], BF16)

    @pl.when(t == last)
    def _():
        for ref in (ge, gp):
            ref[2:4] = jnp.zeros((2,) + ref.shape[1:], BF16)

    pl.semaphore_wait(barrier, len(partners))

    def message(slot, src, dst, target):
        return pltpu.make_async_remote_copy(
            src_ref=src,
            dst_ref=dst,
            send_sem=hs.at[slot],
            recv_sem=hr.at[slot],
            device_id=target,
            device_id_type=MESH,
        )

    def same(slot, ref, target):
        return message(slot, ref, ref, target)

    own, ahead = pl.ds(2, 2), pl.ds(0, 2)
    x_core = same(0, xe.at[own, rows], core)
    g_core = same(1, ge.at[ahead, rows], core)
    x_later = message(2, xe.at[own, rows], xe.at[ahead, rows], later)
    g_earlier = message(3, ge.at[ahead, rows], ge.at[own, rows], earlier)
    x_halo_core = same(4, xe.at[ahead, rows], core)
    g_halo_core = same(5, ge.at[own, rows], core)
    xp_own = message(6, xe.at[own, rows, :, half(1 - ybit)], xp.at[own, rows], ydev)
    xp_own_core = same(7, xp.at[own, rows], core)
    xp_halo = message(8, xe.at[ahead, rows, :, half(1 - ybit)], xp.at[ahead, rows], ydev)
    xp_halo_core = same(9, xp.at[ahead, rows], core)
    gp_own = message(10, ge.at[ahead, rows], gp.at[ahead, rows], xdev)
    gp_own_core = same(11, gp.at[ahead, rows], core)
    gp_halo = message(12, ge.at[own, rows], gp.at[own, rows], xdev)
    gp_halo_core = same(13, gp.at[own, rows], core)
    d_core = same(14, de.at[:, own_rows], core)
    d_pair = message(15, de.at[:, own_rows], dp.at[:, own_rows], ydev)
    d_pair_core = same(16, dp.at[:, own_rows], core)
    h_core = same(17, he.at[own, rows], core)
    h_later = message(18, he.at[own, rows], he.at[ahead, rows], later)
    h_halo_core = same(19, he.at[ahead, rows], core)
    h_pair = message(20, he.at[own, rows, :, half(1 - xbit)], hp.at[:, own_rows], xdev)
    h_pair_core = same(21, hp.at[:, own_rows], core)

    def when(cond, action):
        pl.when(cond)(action)

    inner, outer = t > 0, t < last
    when(outer, lambda: x_later.start())
    when(inner, lambda: g_earlier.start())
    x_core.start()
    g_core.start()
    gp_own.start()
    xp_own.start()

    def shifted(value, by):
        count = value.shape[0]
        column = lax.broadcasted_iota(jnp.int32, value.shape, 0) % wide
        moved = pltpu.roll(value, by % count, axis=0)
        return jnp.where(column == (0 if by == 1 else wide - 1), 0.0, moved)

    def partial_conv(src, weight, taps, transposed, fresh):
        for e in range(3):
            total = None
            for a in taps:
                first = 2 - a if transposed else a
                for b in range(3):
                    down = 2 - b if transposed else b
                    slab = src[first : first + 2, pl.ds(base + down, tall)].reshape(spots, chans)
                    dims = (((1,), (1 if transposed else 0,)), ((), ()))
                    term = lax.dot_general(slab, weight[9 * a + 3 * b + e], dims, preferred_element_type=F32)
                    total = term if total is None else total + term
            if fresh:
                ys[e] = total
            else:
                ys[e] = ys[e] + total

    def joined(transposed):
        one = -1 if transposed else 1
        return ys[1] + shifted(ys[0], one) + shifted(ys[2], -one)

    w_enc.wait()
    x_core.wait_recv()
    partial_conv(xe, wenc, (2,), False, True)

    @pl.when(inner)
    def _():
        x_later.wait_recv()
        x_halo_core.start()
        xp_halo.start()
        x_halo_core.wait_recv()

    partial_conv(xe, wenc, (1, 0), False, False)
    pre = joined(False)
    sig = jax.nn.sigmoid(pre)
    hidden = (pre * sig).astype(BF16)
    slope[...] = sig * (1.0 + pre * (1.0 - sig))
    he[2:4, rows] = hidden.reshape(frames, tall, wide, chans)
    h_pair.start()
    h_core.start()
    when(outer, lambda: h_later.start())

    @pl.when(outer)
    def _():
        g_earlier.wait_recv()
        g_halo_core.start()
        gp_halo.start()

    xp_own.wait_recv()
    xp_own_core.start()
    gp_own.wait_recv()
    gp_own_core.start()
    g_core.wait_recv()
    w_dec.wait()
    when(outer, lambda: g_halo_core.wait_recv())
    partial_conv(ge, wdec, (2, 1, 0), True, True)
    de[:, own_rows] = (joined(True) * slope[...]).astype(BF16).reshape(frames, tall, wide, chans)
    d_pair.start()
    d_core.start()

    chip = 2 * spots

    def turned(value, at):
        value = value.astype(F32)
        for e in range(3):
            moved = value if e == 1 else shifted(value, 1 if e == 0 else -1)
            ht[pl.ds(128 * e, 128), pl.ds(at * chip, chip)] = moved.T.astype(BF16)

    h_core.wait_recv()
    turned(he[2:4, 1:9, :, half(xbit)].reshape(chip, 128), 0)
    h_pair.wait_recv()
    h_pair_core.start()

    def forward_gp():
        gp_halo.wait_recv()
        gp_halo_core.start()

    def forward_xp():
        xp_halo.wait_recv()
        xp_halo_core.start()

    when(outer, forward_gp)
    when(inner, forward_xp)
    h_pair_core.wait_recv()
    turned(hp[...].reshape(chip, 128), 1)
    gp_own_core.wait_recv()
    xp_own_core.wait_recv()
    when(outer, lambda: gp_halo_core.wait_recv())
    when(inner, lambda: xp_halo_core.wait_recv())

    def spread(value, at):
        value = value.astype(F32)
        for e in range(3):
            moved = value if e == 1 else shifted(value, -1 if e == 0 else 1)
            ds[at, :, :, :, pl.ds(chans * e, chans)] = moved.astype(BF16).reshape(frames, 8, wide, chans)

    def kind(i, hh):
        enc = jnp.where((i == 2) | (i == 4) | (i == 6) | (i == 7), 1, 0)
        enc = jnp.where(i == 8, hh, enc)
        before = jnp.where(i > 2, 1, 0) + jnp.where(i > 4, 1, 0) + jnp.where(i > 6, 1, 0) + jnp.where(i > 7, 1, 0)
        tap = jnp.where(enc == 1, before + 4 * hh, i - before + 5 * hh)
        return enc, tap

    def places(i):
        enc, tap = kind(i, h)
        f1 = jnp.where(enc == 1, ybit, xbit)
        f2 = jnp.where(enc == 1, xbit, ybit)
        dx, dy = d + 1 - 2 * xbit, d + 2 - 4 * ybit
        p1 = (jnp.where(enc == 1, dy, dx), t, h)
        p2 = (jnp.where(enc == 1, dx, dy), t, h)
        return 9 * enc + tap, f1, f2, p1, p2

    def copy(i, slot, src, dst, target):
        return pltpu.make_async_remote_copy(
            src_ref=src,
            dst_ref=dst,
            send_sem=ssem.at[i, slot],
            recv_sem=rsem.at[i, slot],
            device_id=target,
            device_id_type=MESH,
        )

    def part(ref, i, first, count):
        return ref.at[i, :, pl.ds(pl.multiple_of(first, 16), count)]

    def zmate(k):
        return lax.rem(t + k, last + 1)

    def c_second(i):
        _, _, _, _, p2 = places(i)
        return copy(i, 0, give.at[i], r1.at[i], p2)

    def c_z(i, k):
        other = zmate(k)
        return copy(i, k, part(zb, i, 16 * other, 16), rz.at[i, k - 1], (d, other, h))

    def c_zback(i, k):
        s, f1, f2, _, _ = places(i)
        here = part(out, s, 128 * f1 + 64 * f2 + 16 * t, 16)
        return copy(i, 3 + k, here, here, (d, zmate(k), h))

    def c_secondback(i):
        s, f1, f2, _, p2 = places(i)
        here = part(out, s, 128 * f1 + 64 * f2, 64)
        return copy(i, 7, here, here, p2)

    def c_firstback(i):
        s, f1, _, p1, _ = places(i)
        here = part(out, s, 128 * f1, 128)
        return copy(i, 8, here, here, p1)

    def c_coreback(i, k):
        s, f1, _, _, _ = places(i)
        here = part(out, s, 128 * (f1 if k == 0 else 1 - f1), 128)
        return copy(i, 9 + k, here, here, core)

    def dec_slab(tap):
        a = tap // 3
        b = tap % 3
        total = None
        for at, ref in ((0, ge), (1, gp)):
            slab = ref[pl.ds(2 - a, 2), pl.ds(2 - b, 8)].reshape(chip, chans)
            term = jnp.dot(ht[:, at * chip : (at + 1) * chip], slab, preferred_element_type=F32)
            total = term if total is None else total + term
        for e in range(3):
            yb[e] = total[128 * e : 128 * (e + 1)]

    def enc_slab(tap):
        a = tap // 3
        b = tap % 3
        total = None
        for at in range(2):
            if at == 0:
                slab = xe[pl.ds(a, 2), pl.ds(b, 8), :, half(ybit)]
            else:
                slab = xp[pl.ds(a, 2), pl.ds(b, 8)]
            term = lax.dot_general(
                slab.reshape(chip, 128),
                ds[at].reshape(chip, 3 * chans),
                (((0,), (0,)), ((), ())),
                preferred_element_type=F32,
            )
            total = term if total is None else total + term
        for e in range(3):
            yb[e] = total[:, chans * e : chans * (e + 1)]

    def s0(i):
        enc, tap = kind(i, h)

        @pl.when(i == 2)
        def _():
            d_core.wait_recv()
            spread(de[...].reshape(chip, chans), 0)
            d_pair.wait_recv()
            d_pair_core.start()
            d_pair_core.wait_recv()
            spread(dp[...].reshape(chip, chans), 1)

        @pl.when(enc == 0)
        def _():
            dec_slab(tap)

        @pl.when(enc == 1)
        def _():
            enc_slab(tap)

        _, _, f2, _, _ = places(i)
        keep[i] = yb[:, pl.ds(pl.multiple_of(64 * f2, 64), 64)]
        give[i] = yb[:, pl.ds(pl.multiple_of(64 * (1 - f2), 64), 64)].astype(BF16)
        c_second(i).start()

        @pl.when(i == 1)
        def _():
            @pl.when(inner)
            def _():
                h_later.wait_recv()
                h_halo_core.start()

        @pl.when(i == 4)
        def _():
            @pl.when(inner)
            def _():
                h_halo_core.wait_recv()

            partial_conv(he, wdec, (0, 1, 2), False, True)
            total = joined(False) + xe[2:4, rows].reshape(spots, chans).astype(F32)
            output[0] = total.astype(BF16).reshape(frames, tall, wide, chans)

    def s1(i):
        c_second(i).wait_recv()
        total = keep[i] + r1[i].astype(F32)
        keep[i] = total
        zb[i] = total.astype(BF16)
        for k in (2, 1, 3):
            c_z(i, k).start()

    def s2(i):
        s, f1, f2, _, _ = places(i)
        for k in (1, 2, 3):
            c_z(i, k).wait_recv()
        total = keep[i, :, pl.ds(pl.multiple_of(16 * t, 16), 16)]
        for k in range(3):
            total = total + rz[i, k].astype(F32)
        out[s, :, pl.ds(pl.multiple_of(128 * f1 + 64 * f2 + 16 * t, 16), 16)] = total.astype(BF16)
        for k in (2, 1, 3):
            c_zback(i, k).start()

    def s3(i):
        for k in (1, 2, 3):
            c_zback(i, k).wait_recv()
        c_secondback(i).start()

    def s4(i):
        c_secondback(i).wait_recv()
        c_firstback(i).start()
        c_coreback(i, 0).start()

    def s5(i):
        c_firstback(i).wait_recv()
        c_coreback(i, 1).start()

    def s6(i):
        c_coreback(i, 0).wait_recv()
        c_coreback(i, 1).wait_recv()

    stages = [s0, s1, s2, s3, s4, s5, s6]

    def body(i, carry):
        for k in (0, 6, 5, 4, 3, 2, 1):
            s = i - LAG * k

            @pl.when((s >= 0) & (s < STEPS))
            def _(k=k, s=s):
                stages[k](s)

        return carry

    lax.fori_loop(0, STEPS + LAG * (len(stages) - 1), body, 0)

    def finish(i, carry):
        c_second(i).wait_send()
        for k in (1, 2, 3):
            c_z(i, k).wait_send()
            c_zback(i, k).wait_send()
        c_secondback(i).wait_send()
        c_firstback(i).wait_send()
        c_coreback(i, 0).wait_send()
        c_coreback(i, 1).wait_send()
        return carry

    lax.fori_loop(0, STEPS, finish, 0)
    for sent in (x_core, g_core, xp_own, xp_own_core, gp_own, gp_own_core, d_core, d_pair, d_pair_core,
                 h_core, h_pair, h_pair_core):
        sent.wait_send()

    @pl.when(inner)
    def _():
        for sent in (g_earlier, x_halo_core, xp_halo, xp_halo_core, h_halo_core):
            sent.wait_send()

    @pl.when(outer)
    def _():
        for sent in (x_later, h_later, g_halo_core, gp_halo, gp_halo_core):
            sent.wait_send()


def whole_step(video, lengths, enc_weight, dec_weight, cotangent):
    vmem, bf = pltpu.VMEM, BF16
    frames, tall, wide, chans = video.shape[1:]
    spots = frames * tall * wide
    ext = (4, 10, wide, chans)
    enc27, dec27 = (w.reshape(27, chans, chans) for w in (enc_weight, dec_weight))
    output, grads = pl.pallas_call(
        step_kernel,
        out_shape=[
            jax.ShapeDtypeStruct(video.shape, bf),
            jax.ShapeDtypeStruct((18, 3, chans, chans), bf),
        ],
        in_specs=[
            pl.BlockSpec(memory_space=pltpu.SMEM),
            pl.BlockSpec(memory_space=vmem),
            pl.BlockSpec(memory_space=vmem),
            pl.BlockSpec(memory_space=pl.ANY),
            pl.BlockSpec(memory_space=pl.ANY),
        ],
        out_specs=[pl.BlockSpec(memory_space=vmem)] * 2,
        scratch_shapes=[
            vmem((27, chans, chans), bf),
            vmem((27, chans, chans), bf),
            vmem(ext, bf),
            vmem(ext, bf),
            vmem(ext, bf),
            vmem((frames, 8, wide, chans), bf),
            vmem((4, 10, wide, 128), bf),
            vmem(ext, bf),
            vmem((frames, 8, wide, 128), bf),
            vmem((frames, 8, wide, chans), bf),
            vmem((384, 4 * spots), bf),
            vmem((2, frames, 8, wide, 3 * chans), bf),
            vmem((3, spots, chans), F32),
            vmem((spots, chans), F32),
            vmem((3, 128, chans), F32),
            vmem((STEPS, 3, 64, chans), F32),
            vmem((STEPS, 3, 64, chans), bf),
            vmem((STEPS, 3, 64, chans), bf),
            vmem((STEPS, 3, 64, chans), bf),
            vmem((STEPS, 3, 3, 16, chans), bf),
            pltpu.SemaphoreType.DMA((2,)),
            pltpu.SemaphoreType.DMA((22,)),
            pltpu.SemaphoreType.DMA((22,)),
            pltpu.SemaphoreType.DMA((STEPS, 11)),
            pltpu.SemaphoreType.DMA((STEPS, 11)),
        ],
        compiler_params=pltpu.CompilerParams(
            collective_id=0, has_side_effects=True, vmem_limit_bytes=56 * 2**20
        ),
    )(lengths, video, cotangent, enc27, dec27)
    dec_grad = grads[:9].astype(F32).reshape(dec_weight.shape)
    enc_grad = grads[9:].astype(F32).reshape(enc_weight.shape)
    return output, enc_grad, dec_grad


def shards(video, lengths, enc_weight, dec_weight, cotangent):
    sizes = tuple(lax.axis_size(axis) for axis in ("dp", "tm", "height"))
    if sizes == (4, 4, 2) and video.shape[:3] == (1, 2, 4) and video.shape[-1] == 256:
        return whole_step(video, lengths, enc_weight, dec_weight, cotangent)
    frames = video.shape[1]
    first_frame = lax.axis_index("tm") * frames
    tpos = first_frame + jnp.arange(frames, dtype=jnp.int32)
    keep = (tpos[None, :] < lengths[:, None])[:, :, None, None, None]
    masked = jnp.where(keep, video, jnp.zeros_like(video))
    cot_masked = jnp.where(keep, cotangent, jnp.zeros_like(cotangent))
    ext_x = with_earlier(masked)
    pre = apply_taps(ext_x, enc_weight)
    hidden = jax.nn.silu(pre).astype(jnp.bfloat16)
    ext_h = with_earlier(hidden)
    output = (apply_taps(ext_h, dec_weight) + masked.astype(jnp.float32)).astype(jnp.bfloat16)
    ext_g = with_later(cot_masked)
    chans = dec_weight.shape[3]
    flipped = jnp.transpose(dec_weight[::-1, ::-1, ::-1], (0, 1, 3, 2, 4)).reshape(3, 3, chans, -1)
    dec_local = tap_grads(ext_h, cot_masked)
    back = apply_taps(ext_g, flipped, True)
    dpre = (back * dsilu(pre)).astype(jnp.bfloat16)
    enc_local = tap_grads(ext_x, dpre)
    enc_grad, dec_grad = sum_all(enc_local), sum_all(dec_local)
    return (output, enc_grad, dec_grad)


def solution(mesh):
    in_specs = (
        P("dp", "tm", "height", None, None),
        P("dp"),
        P(),
        P(),
        P("dp", "tm", "height", None, None),
    )
    out_specs = (P("dp", "tm", "height", None, None), P(), P())
    return jax.shard_map(shards, mesh=mesh, in_specs=in_specs, out_specs=out_specs, check_vma=False)
```

profile of v0, /device:TPU:1, one launch (start us, length us, event | category | flops | bytes accessed | tf_op | source)
XLA Modules:
  0.0 121.0 jit_solution(6557260445996046823)
XLA Ops:
  1.3 107.8 %shard_map.76 = (bf16[1,2,4,64,256]{4,3,2,1,0:T(8,128)(2,1)}, bf16[18,3,256,256]{3,2,1,0:T(8,128)(2,1)}) custom-call(s32[1]{0:T(128)S(6)} %copy.9.lengths, bf16[1,2,4,64,256]{4,3,2,1,0:T(8,128)(2,1)} %video.1, bf16[1,2,4,64,256]{4,3,2,1,0:T(8,128)(2,1)} %cot.1, bf16[27,256,256]{2,1,0:T(8,128)(2,1)} %bitcast.8, bf16[27,256,256]{2,1,0:T(8,128)(2,1)} %bitcast.9), custom_call_target="tpu_custom_call" | custom-call | tf_op jit(solution)/shard_map/pallas_call | solution.py:557
  109.1 3.5 %fusion = (bf16[9,3,256,256]{3,2,1,0:T(8,128)(2,1)S(1)}, bf16[9,3,256,256]{3,2,1,0:T(8,128)(2,1)S(1)}) fusion(bf16[18,3,256,256]{3,2,1,0:T(8,128)(2,1)} %get-tuple-element.6), kind=kLoop, calls=%fused_computation | loop fusion | bytes 14155776 | tf_op jit(solution)/shard_map/slice | solution.py:602
  112.7 3.8 %convert.2 = f32[3,3,3,256,256]{4,3,2,1,0:T(8,128)} convert(bf16[3,3,3,256,256]{4,3,2,1,0:T(8,128)(2,1)S(1)} %bitcast.7) | non-fusion elementwise | flops 1769472 | bytes 10616832 | tf_op jit(solution)/shard_map/reshape | solution.py:603
  116.5 0.0 copy-start
  116.5 3.8 %convert.3 = f32[3,3,3,256,256]{4,3,2,1,0:T(8,128)} convert(bf16[3,3,3,256,256]{4,3,2,1,0:T(8,128)(2,1)S(1)} %bitcast.6) | non-fusion elementwise | flops 1769472 | bytes 10616832 | tf_op jit(solution)/shard_map/reshape | solution.py:602
  120.3 0.0 copy-done
  120.3 0.7 copy.10
Async XLA Ops:
  116.5 3.8 %copy-start = (bf16[1,2,4,64,256]{4,3,2,1,0:T(8,128)(2,1)S(1)}, bf16[1,2,4,64,256]{4,3,2,1,0:T(8,128)(2,1)}, u32[]{:S(2)}) copy-start(bf16[1,2,4,64,256]{4,3,2,1,0:T(8,128)(2,1)} %get-tuple-element.12) | copy-start | bytes 786436
where the time goes:
time: 122 us; the launch traced here: 121 us
  Pallas kernels  108 us (89%)
  other arithmetic  7.66 us (6%)
  local copies, waits for them, and re-layouts  4.24 us (3%)
  between operations  1.29 us (1%)
    pallas_call x1, Pallas kernels, whole_step(): pl.pallas_call(step_kernel, out_shape=[jax.ShapeDtypeStruct(video.shape,...  108 us
    reshape x1, other arithmetic, whole_step(): enc_grad = grads[9:].astype(F32).reshape(enc_weight.shape)  3.83 us
    reshape x1, other arithmetic, whole_step(): dec_grad = grads[:9].astype(F32).reshape(dec_weight.shape)  3.83 us
    slice x1, local copies, waits for them, and re-layouts, whole_step(): dec_grad = grads[:9].astype(F32).reshape(dec_weight.shape)  3.54 us

commit v1 on v0

--- a/solution.py
+++ b/solution.py
@@ -6,7 +6,7 @@
 from jax.sharding import PartitionSpec as P
 
 MESH = pl.DeviceIdType.MESH
-LAG = 1
+LAG = 3
 
 
 def extended(shard, sides, width):
@@ -131,15 +131,16 @@
         sums.append(sum_part(part, [(2, height[0])] + [(1, bit) for bit in order]))
     return jnp.concatenate(sums, axis=0).reshape(grad.shape)
 
-STEPS = 9
+ITEMS = 9
+STEPS = 2 * ITEMS
 F32 = jnp.float32
 BF16 = jnp.bfloat16
 
 
 def step_kernel(
-    lengths, video, cot, enc_hbm, dec_hbm, output, out,
-    wenc, wdec, xe, ge, he, de, xp, gp, hp, dp, ht, ds, ys, slope,
-    yb, keep, give, r1, zb, rz, wsem, hs, hr, ssem, rsem,
+    lengths, video, cot, enc_hbm, dec_hbm, output, enc_out, dec_out,
+    wenc, wdec, xe, ge, he, de, xp, gp, hp, dp, ht, ds, ys, yg, slope,
+    yb, keep, give, r1, zb, rz, out, wsem, hs, hr, ssem, rsem, lsem,
 ):
     d, t, h = lax.axis_index("dp"), lax.axis_index("tm"), lax.axis_index("height")
     frames, tall, wide, chans = video.shape[1:]
@@ -215,7 +216,7 @@
     xp_halo_core = same(9, xp.at[ahead, rows], core)
     gp_own = message(10, ge.at[ahead, rows], gp.at[ahead, rows], xdev)
     gp_own_core = same(11, gp.at[ahead, rows], core)
-    gp_halo = message(12, ge.at[own, rows], gp.at[own, rows], xdev)
+    gp_halo = message(12, gp.at[ahead, rows], gp.at[own, rows], earlier)
     gp_halo_core = same(13, gp.at[own, rows], core)
     d_core = same(14, de.at[:, own_rows], core)
     d_pair = message(15, de.at[:, own_rows], dp.at[:, own_rows], ydev)
@@ -243,7 +244,7 @@
         moved = pltpu.roll(value, by % count, axis=0)
         return jnp.where(column == (0 if by == 1 else wide - 1), 0.0, moved)
 
-    def partial_conv(src, weight, taps, transposed, fresh):
+    def partial_conv(acc, src, weight, taps, transposed, fresh):
         for e in range(3):
             total = None
             for a in taps:
@@ -255,17 +256,20 @@
                     term = lax.dot_general(slab, weight[9 * a + 3 * b + e], dims, preferred_element_type=F32)
                     total = term if total is None else total + term
             if fresh:
-                ys[e] = total
+                acc[e] = total
             else:
-                ys[e] = ys[e] + total
-
-    def joined(transposed):
+                acc[e] = acc[e] + total
+
+    def joined(acc, transposed):
         one = -1 if transposed else 1
-        return ys[1] + shifted(ys[0], one) + shifted(ys[2], -one)
+        return acc[1] + shifted(acc[0], one) + shifted(acc[2], -one)
 
     w_enc.wait()
     x_core.wait_recv()
-    partial_conv(xe, wenc, (2,), False, True)
+    partial_conv(ys, xe, wenc, (2,), False, True)
+    w_dec.wait()
+    g_core.wait_recv()
+    partial_conv(yg, ge, wdec, (2,), True, True)
 
     @pl.when(inner)
     def _():
@@ -274,8 +278,8 @@
         xp_halo.start()
         x_halo_core.wait_recv()
 
-    partial_conv(xe, wenc, (1, 0), False, False)
-    pre = joined(False)
+    partial_conv(ys, xe, wenc, (1, 0), False, False)
+    pre = joined(ys, False)
     sig = jax.nn.sigmoid(pre)
     hidden = (pre * sig).astype(BF16)
     slope[...] = sig * (1.0 + pre * (1.0 - sig))
@@ -284,21 +288,20 @@
     h_core.start()
     when(outer, lambda: h_later.start())
 
+    gp_own.wait_recv()
+    gp_own_core.start()
+    when(inner, lambda: gp_halo.start())
+    xp_own.wait_recv()
+    xp_own_core.start()
+
     @pl.when(outer)
     def _():
         g_earlier.wait_recv()
         g_halo_core.start()
-        gp_halo.start()
-
-    xp_own.wait_recv()
-    xp_own_core.start()
-    gp_own.wait_recv()
-    gp_own_core.start()
-    g_core.wait_recv()
-    w_dec.wait()
-    when(outer, lambda: g_halo_core.wait_recv())
-    partial_conv(ge, wdec, (2, 1, 0), True, True)
-    de[:, own_rows] = (joined(True) * slope[...]).astype(BF16).reshape(frames, tall, wide, chans)
+        g_halo_core.wait_recv()
+
+    partial_conv(yg, ge, wdec, (1, 0), True, False)
+    de[:, own_rows] = (joined(yg, True) * slope[...]).astype(BF16).reshape(frames, tall, wide, chans)
     d_pair.start()
     d_core.start()
 
@@ -315,22 +318,14 @@
     h_pair.wait_recv()
     h_pair_core.start()
 
-    def forward_gp():
-        gp_halo.wait_recv()
-        gp_halo_core.start()
-
-    def forward_xp():
+    @pl.when(inner)
+    def _():
         xp_halo.wait_recv()
         xp_halo_core.start()
 
-    when(outer, forward_gp)
-    when(inner, forward_xp)
     h_pair_core.wait_recv()
     turned(hp[...].reshape(chip, 128), 1)
     gp_own_core.wait_recv()
-    xp_own_core.wait_recv()
-    when(outer, lambda: gp_halo_core.wait_recv())
-    when(inner, lambda: xp_halo_core.wait_recv())
 
     def spread(value, at):
         value = value.astype(F32)
@@ -339,20 +334,19 @@
             ds[at, :, :, :, pl.ds(chans * e, chans)] = moved.astype(BF16).reshape(frames, 8, wide, chans)
 
     def kind(i, hh):
-        enc = jnp.where((i == 2) | (i == 4) | (i == 6) | (i == 7), 1, 0)
-        enc = jnp.where(i == 8, hh, enc)
-        before = jnp.where(i > 2, 1, 0) + jnp.where(i > 4, 1, 0) + jnp.where(i > 6, 1, 0) + jnp.where(i > 7, 1, 0)
-        tap = jnp.where(enc == 1, before + 4 * hh, i - before + 5 * hh)
+        enc = jnp.where((i == ITEMS - 1) | ((i > 0) & ((i + hh) % 2 == 0)), 1, 0)
+        before = jnp.where(hh == 1, i, jnp.maximum(i - 1, 0)) // 2
+        tap = jnp.where(enc == 1, 7 + hh - 2 * before, 8 - hh - 2 * (i - before))
         return enc, tap
 
     def places(i):
-        enc, tap = kind(i, h)
+        enc, tap = kind(i // 2, h)
         f1 = jnp.where(enc == 1, ybit, xbit)
         f2 = jnp.where(enc == 1, xbit, ybit)
         dx, dy = d + 1 - 2 * xbit, d + 2 - 4 * ybit
         p1 = (jnp.where(enc == 1, dy, dx), t, h)
         p2 = (jnp.where(enc == 1, dx, dy), t, h)
-        return 9 * enc + tap, f1, f2, p1, p2
+        return 18 * enc + 2 * tap + i % 2, f1, f2, p1, p2
 
     def copy(i, slot, src, dst, target):
         return pltpu.make_async_remote_copy(
@@ -407,7 +401,8 @@
             term = jnp.dot(ht[:, at * chip : (at + 1) * chip], slab, preferred_element_type=F32)
             total = term if total is None else total + term
         for e in range(3):
-            yb[e] = total[128 * e : 128 * (e + 1)]
+            for side in range(2):
+                yb[side, e] = total[128 * e : 128 * (e + 1), 128 * side : 128 * (side + 1)]
 
     def enc_slab(tap):
         a = tap // 3
@@ -426,17 +421,29 @@
             )
             total = term if total is None else total + term
         for e in range(3):
-            yb[e] = total[:, chans * e : chans * (e + 1)]
-
-    def s0(i):
+            for side in range(2):
+                at = chans * e + 128 * side
+                yb[side, e] = total[:, at : at + 128]
+
+    def items(i):
         enc, tap = kind(i, h)
 
-        @pl.when(i == 2)
+        @pl.when(i == 1)
+        def _():
+            @pl.when(outer)
+            def _():
+                gp_halo.wait_recv()
+                gp_halo_core.start()
+                gp_halo_core.wait_recv()
+
+        @pl.when(i == 1)
         def _():
             d_core.wait_recv()
             spread(de[...].reshape(chip, chans), 0)
             d_pair.wait_recv()
             d_pair_core.start()
+            xp_own_core.wait_recv()
+            when(inner, lambda: xp_halo_core.wait_recv())
             d_pair_core.wait_recv()
             spread(dp[...].reshape(chip, chans), 1)
 
@@ -447,11 +454,6 @@
         @pl.when(enc == 1)
         def _():
             enc_slab(tap)
-
-        _, _, f2, _, _ = places(i)
-        keep[i] = yb[:, pl.ds(pl.multiple_of(64 * f2, 64), 64)]
-        give[i] = yb[:, pl.ds(pl.multiple_of(64 * (1 - f2), 64), 64)].astype(BF16)
-        c_second(i).start()
 
         @pl.when(i == 1)
         def _():
@@ -466,9 +468,20 @@
             def _():
                 h_halo_core.wait_recv()
 
-            partial_conv(he, wdec, (0, 1, 2), False, True)
-            total = joined(False) + xe[2:4, rows].reshape(spots, chans).astype(F32)
+            partial_conv(ys, he, wdec, (0, 1, 2), False, True)
+            total = joined(ys, False) + xe[2:4, rows].reshape(spots, chans).astype(F32)
             output[0] = total.astype(BF16).reshape(frames, tall, wide, chans)
+
+    def s0(i):
+        @pl.when(i % 2 == 0)
+        def _():
+            items(i // 2)
+
+        _, _, f2, _, _ = places(i)
+        side = i % 2
+        keep[i] = yb[side, :, pl.ds(pl.multiple_of(64 * f2, 64), 64)]
+        give[i] = yb[side, :, pl.ds(pl.multiple_of(64 * (1 - f2), 64), 64)].astype(BF16)
+        c_second(i).start()
 
     def s1(i):
         c_second(i).wait_recv()
@@ -503,14 +516,35 @@
         c_firstback(i).wait_recv()
         c_coreback(i, 1).start()
 
+    def leave(i, hh, action):
+        enc, tap = kind(i // 2, hh)
+        side = i % 2
+        s = 18 * enc + 2 * tap + side
+        slot = jnp.where(hh == h, 0, 1)
+
+        def to(dst):
+            return pltpu.make_async_copy(
+                out.at[s], dst.at[pl.ds(3 * tap, 3), :, pl.ds(pl.multiple_of(128 * side, 128), 128)], lsem.at[i, slot]
+            )
+
+        @pl.when(enc == 1)
+        def _():
+            action(to(enc_out))
+
+        @pl.when(enc == 0)
+        def _():
+            action(to(dec_out))
+
     def s6(i):
         c_coreback(i, 0).wait_recv()
         c_coreback(i, 1).wait_recv()
+        leave(i, h, lambda c: c.start())
+        leave(i, 1 - h, lambda c: c.start())
 
     stages = [s0, s1, s2, s3, s4, s5, s6]
 
     def body(i, carry):
-        for k in (0, 6, 5, 4, 3, 2, 1):
+        for k in (6, 5, 4, 3, 2, 1, 0):
             s = i - LAG * k
 
             @pl.when((s >= 0) & (s < STEPS))
@@ -530,6 +564,8 @@
         c_firstback(i).wait_send()
         c_coreback(i, 0).wait_send()
         c_coreback(i, 1).wait_send()
+        leave(i, h, lambda c: c.wait())
+        leave(i, 1 - h, lambda c: c.wait())
         return carry
 
     lax.fori_loop(0, STEPS, finish, 0)
@@ -539,12 +575,12 @@
 
     @pl.when(inner)
     def _():
-        for sent in (g_earlier, x_halo_core, xp_halo, xp_halo_core, h_halo_core):
+        for sent in (g_earlier, x_halo_core, xp_halo, xp_halo_core, gp_halo, h_halo_core):
             sent.wait_send()
 
     @pl.when(outer)
     def _():
-        for sent in (x_later, h_later, g_halo_core, gp_halo, gp_halo_core):
+        for sent in (x_later, h_later, g_halo_core, gp_halo_core):
             sent.wait_send()
 
 
@@ -554,11 +590,12 @@
     spots = frames * tall * wide
     ext = (4, 10, wide, chans)
     enc27, dec27 = (w.reshape(27, chans, chans) for w in (enc_weight, dec_weight))
-    output, grads = pl.pallas_call(
+    output, enc_grad, dec_grad = pl.pallas_call(
         step_kernel,
         out_shape=[
             jax.ShapeDtypeStruct(video.shape, bf),
-            jax.ShapeDtypeStruct((18, 3, chans, chans), bf),
+            jax.ShapeDtypeStruct((27, chans, chans), bf),
+            jax.ShapeDtypeStruct((27, chans, chans), bf),
         ],
         in_specs=[
             pl.BlockSpec(memory_space=pltpu.SMEM),
@@ -567,7 +604,7 @@
             pl.BlockSpec(memory_space=pl.ANY),
             pl.BlockSpec(memory_space=pl.ANY),
         ],
-        out_specs=[pl.BlockSpec(memory_space=vmem)] * 2,
+        out_specs=[pl.BlockSpec(memory_space=vmem)] + [pl.BlockSpec(memory_space=pl.ANY)] * 2,
         scratch_shapes=[
             vmem((27, chans, chans), bf),
             vmem((27, chans, chans), bf),
@@ -582,25 +619,27 @@
             vmem((384, 4 * spots), bf),
             vmem((2, frames, 8, wide, 3 * chans), bf),
             vmem((3, spots, chans), F32),
+            vmem((3, spots, chans), F32),
             vmem((spots, chans), F32),
-            vmem((3, 128, chans), F32),
-            vmem((STEPS, 3, 64, chans), F32),
-            vmem((STEPS, 3, 64, chans), bf),
-            vmem((STEPS, 3, 64, chans), bf),
-            vmem((STEPS, 3, 64, chans), bf),
-            vmem((STEPS, 3, 3, 16, chans), bf),
+            vmem((2, 3, 128, 128), F32),
+            vmem((STEPS, 3, 64, 128), F32),
+            vmem((STEPS, 3, 64, 128), bf),
+            vmem((STEPS, 3, 64, 128), bf),
+            vmem((STEPS, 3, 64, 128), bf),
+            vmem((STEPS, 3, 3, 16, 128), bf),
+            vmem((36, 3, chans, 128), bf),
             pltpu.SemaphoreType.DMA((2,)),
             pltpu.SemaphoreType.DMA((22,)),
             pltpu.SemaphoreType.DMA((22,)),
             pltpu.SemaphoreType.DMA((STEPS, 11)),
             pltpu.SemaphoreType.DMA((STEPS, 11)),
+            pltpu.SemaphoreType.DMA((STEPS, 2)),
         ],
         compiler_params=pltpu.CompilerParams(
             collective_id=0, has_side_effects=True, vmem_limit_bytes=56 * 2**20
         ),
     )(lengths, video, cotangent, enc27, dec27)
-    dec_grad = grads[:9].astype(F32).reshape(dec_weight.shape)
-    enc_grad = grads[9:].astype(F32).reshape(enc_weight.shape)
+    enc_grad, dec_grad = (g.astype(F32).reshape(enc_weight.shape) for g in (enc_grad, dec_grad))
     return output, enc_grad, dec_grad
 
 

time: 122 us -> 99.5 us (0.82)
  Pallas kernels: 108 us -> 87.5 us
  local copies, waits for them, and re-layouts: 4.24 us -> 0.71 us
  other arithmetic: 7.66 us -> 9.83 us
    pallas_call x1, Pallas kernels: 108 us -> 87.5 us  [whole_step(): pl.pallas_call(step_kernel, out_shape=[jax.ShapeDtypeStruct(video.shape,...]
    slice x1 -> x0, local copies, waits for them, and re-layouts: 3.54 us -> none  [whole_step(): dec_grad = grads[:9].astype(F32).reshape(dec_weight.shape)]
    reshape x2, other arithmetic: 7.66 us -> 9.83 us  [whole_step(): g.astype(F32).reshape(enc_weight.shape)]
where the time goes in v1:
time: 99.5 us; the launch traced here: 99.3 us
  Pallas kernels  87.5 us (88%)
  other arithmetic  9.83 us (10%)
  between operations  1.3 us (1%)
    pallas_call x1, Pallas kernels, whole_step(): pl.pallas_call(step_kernel, out_shape=[jax.ShapeDtypeStruct(video.shape,...  87.5 us
    reshape x2, other arithmetic, whole_step(): g.astype(F32).reshape(enc_weight.shape)  9.83 us

profile of v1, /device:TPU:1, one launch (start us, length us, event | category | flops | bytes accessed | tf_op | source)
XLA Modules:
  0.0 99.3 jit_solution(1040515217820766732)
XLA Ops:
  1.3 87.5 %shard_map.76 = (bf16[1,2,4,64,256]{4,3,2,1,0:T(8,128)(2,1)}, bf16[27,256,256]{2,1,0:T(8,128)(2,1)}, bf16[27,256,256]{2,1,0:T(8,128)(2,1)}) custom-call(s32[1]{0:T(128)S(6)} %copy.9.lengths, bf16[1,2,4,64,256]{4,3,2,1,0:T(8,128)(2,1)} %video.1, bf16[1,2,4,64,256]{4,3,2,1,0:T(8,128)(2,1)} %cot.1, bf16[27,256,256]{2,1,0:T(8,128)(2,1)} %bitcast.6, ...), custom_call_target="tpu_custom_call" | custom-call | tf_op jit(solution)/shard_map/pallas_call | solution.py:593
  88.8 0.0 copy-start
  88.8 6.0 %convert.2 = f32[3,3,3,256,256]{4,3,2,1,0:T(8,128)} convert(bf16[3,3,3,256,256]{4,3,2,1,0:T(8,128)(2,1)} %bitcast.9) | non-fusion elementwise | flops 1769472 | bytes 10616832 | tf_op jit(solution)/shard_map/reshape | solution.py:642
  94.8 0.0 copy-done
  94.8 0.0 copy-start.1
  94.8 3.8 %convert.3 = f32[3,3,3,256,256]{4,3,2,1,0:T(8,128)} convert(bf16[3,3,3,256,256]{4,3,2,1,0:T(8,128)(2,1)S(1)} %bitcast.8) | non-fusion elementwise | flops 1769472 | bytes 10616832 | tf_op jit(solution)/shard_map/reshape | solution.py:642
  98.6 0.0 copy-done.1
  98.6 0.7 copy.10
Async XLA Ops:
  88.8 6.0 %copy-start = (bf16[27,256,256]{2,1,0:T(8,128)(2,1)S(1)}, bf16[27,256,256]{2,1,0:T(8,128)(2,1)}, u32[]{:S(2)}) copy-start(bf16[27,256,256]{2,1,0:T(8,128)(2,1)} %get-tuple-element.8) | copy-start | bytes 10616836
  94.8 3.8 %copy-start.1 = (bf16[1,2,4,64,256]{4,3,2,1,0:T(8,128)(2,1)S(1)}, bf16[1,2,4,64,256]{4,3,2,1,0:T(8,128)(2,1)}, u32[]{:S(2)}) copy-start(bf16[1,2,4,64,256]{4,3,2,1,0:T(8,128)(2,1)} %get-tuple-element.12) | copy-start | bytes 786436

commit v2 on v1

--- a/solution.py
+++ b/solution.py
@@ -6,7 +6,8 @@
 from jax.sharding import PartitionSpec as P
 
 MESH = pl.DeviceIdType.MESH
-LAG = 3
+ORDER = (8, 7, 6, 5, 4, 3, 2, 1, 0)
+LAGS = (0, 5, 8, 12, 15, 17, 21, 25, 28)
 
 
 def extended(shard, sides, width):
@@ -140,7 +141,7 @@
 def step_kernel(
     lengths, video, cot, enc_hbm, dec_hbm, output, enc_out, dec_out,
     wenc, wdec, xe, ge, he, de, xp, gp, hp, dp, ht, ds, ys, yg, slope,
-    yb, keep, give, r1, zb, rz, out, wsem, hs, hr, ssem, rsem, lsem,
+    yb, keep, give, r1, zb, zc, ra, rn, rc, out, wsem, hs, hr, ssem, rsem, lsem,
 ):
     d, t, h = lax.axis_index("dp"), lax.axis_index("tm"), lax.axis_index("height")
     frames, tall, wide, chans = video.shape[1:]
@@ -174,20 +175,6 @@
         live = t * frames + f < lengths[0]
         xe[2 + f, rows] = jnp.where(live, video[0, f], jnp.zeros_like(video[0, f]))
         ge[f, rows] = jnp.where(live, cot[0, f], jnp.zeros_like(cot[0, f]))
-    for ref in (xe, ge, he, xp, gp):
-        for edge in (0, 9):
-            ref[:, edge] = jnp.zeros((4,) + ref.shape[2:], BF16)
-
-    @pl.when(t == 0)
-    def _():
-        for ref in (xe, he, xp):
-            ref[0:2] = jnp.zeros((2,) + ref.shape[1:], BF16)
-
-    @pl.when(t == last)
-    def _():
-        for ref in (ge, gp):
-            ref[2:4] = jnp.zeros((2,) + ref.shape[1:], BF16)
-
     pl.semaphore_wait(barrier, len(partners))
 
     def message(slot, src, dst, target):
@@ -238,6 +225,20 @@
     gp_own.start()
     xp_own.start()
 
+    for ref in (xe, ge, he, xp, gp):
+        for edge in (0, 9):
+            ref[:, edge] = jnp.zeros((4,) + ref.shape[2:], BF16)
+
+    @pl.when(t == 0)
+    def _():
+        for ref in (xe, he, xp):
+            ref[0:2] = jnp.zeros((2,) + ref.shape[1:], BF16)
+
+    @pl.when(t == last)
+    def _():
+        for ref in (ge, gp):
+            ref[2:4] = jnp.zeros((2,) + ref.shape[1:], BF16)
+
     def shifted(value, by):
         count = value.shape[0]
         column = lax.broadcasted_iota(jnp.int32, value.shape, 0) % wide
@@ -334,8 +335,9 @@
             ds[at, :, :, :, pl.ds(chans * e, chans)] = moved.astype(BF16).reshape(frames, 8, wide, chans)
 
     def kind(i, hh):
-        enc = jnp.where((i == ITEMS - 1) | ((i > 0) & ((i + hh) % 2 == 0)), 1, 0)
-        before = jnp.where(hh == 1, i, jnp.maximum(i - 1, 0)) // 2
+        start = ITEMS // 2 + 1 - hh
+        enc = jnp.where(i >= start, 1, 0)
+        before = jnp.maximum(i - start, 0)
         tap = jnp.where(enc == 1, 7 + hh - 2 * before, 8 - hh - 2 * (i - before))
         return enc, tap
 
@@ -361,36 +363,66 @@
     def part(ref, i, first, count):
         return ref.at[i, :, pl.ds(pl.multiple_of(first, 16), count)]
 
-    def zmate(k):
-        return lax.rem(t + k, last + 1)
+    edge = (t == 0) | (t == last)
+    near = jnp.where(t == 0, 1, 2)
+    side_edge = jnp.where(t == 1, 0, last)
+
+    def along(other):
+        return (d, other, h)
 
     def c_second(i):
         _, _, _, _, p2 = places(i)
         return copy(i, 0, give.at[i], r1.at[i], p2)
 
-    def c_z(i, k):
-        other = zmate(k)
-        return copy(i, k, part(zb, i, 16 * other, 16), rz.at[i, k - 1], (d, other, h))
-
-    def c_zback(i, k):
+    def c_hand(i):
+        return copy(i, 1, part(zb, i, jnp.where(t == 0, 16, 0), 48), ra.at[i], along(near))
+
+    def c_near(i):
+        return copy(i, 1, part(zb, i, 16 * side_edge, 16), rn.at[i], along(side_edge))
+
+    def c_cross(i):
+        return copy(i, 2, part(zc, i, jnp.where(t == 1, 0, 16), 16), rc.at[i], along(last - t))
+
+    def c_far(i):
+        return copy(i, 3, part(zc, i, jnp.where(t == 1, 16, 0), 16), rc.at[i], along(last - side_edge))
+
+    def shard(i, owner, count=1):
         s, f1, f2, _, _ = places(i)
-        here = part(out, s, 128 * f1 + 64 * f2 + 16 * t, 16)
-        return copy(i, 3 + k, here, here, (d, zmate(k), h))
-
-    def c_secondback(i):
-        s, f1, f2, _, p2 = places(i)
-        here = part(out, s, 128 * f1 + 64 * f2, 64)
-        return copy(i, 7, here, here, p2)
-
-    def c_firstback(i):
-        s, f1, _, p1, _ = places(i)
-        here = part(out, s, 128 * f1, 128)
-        return copy(i, 8, here, here, p1)
-
-    def c_coreback(i, k):
-        s, f1, _, _, _ = places(i)
-        here = part(out, s, 128 * (f1 if k == 0 else 1 - f1), 128)
-        return copy(i, 9 + k, here, here, core)
+        return part(out, s, 128 * f1 + 64 * f2 + 16 * owner, 16 * count)
+
+    def c_shard(i, slot, other):
+        return copy(i, slot, shard(i, t), shard(i, t), along(other))
+
+    def c_arrive(i, slot, owner, count=1):
+        return copy(i, slot, shard(i, owner, count), shard(i, owner, count), along(owner))
+
+    def c_pass(i):
+        here = shard(i, jnp.where(t == 1, 2, 0), 2)
+        return copy(i, 5, here, here, along(side_edge))
+
+    def piece(i, flip1, flip2, first, count):
+        s, f1, f2, _, _ = places(i)
+        g1, g2 = (1 - f1 if flip1 else f1), (1 - f2 if flip2 else f2)
+        return part(out, s, 128 * g1 + 64 * g2 + first, count)
+
+    def gather(i, slot, here, which):
+        return copy(i, slot, here, here, places(i)[which])
+
+    def c_own2(i):
+        return gather(i, 7, piece(i, False, False, 0, 64), 4)
+
+    def c_own1(i):
+        return gather(i, 8, piece(i, False, False, 0, 64), 3)
+
+    def c_on1(i):
+        return gather(i, 9, piece(i, False, True, 0, 32), 3)
+
+    def c_on2(i):
+        return gather(i, 10, piece(i, True, False, 32, 32), 4)
+
+    def c_coreback(i):
+        s = places(i)[0]
+        return copy(i, 11, out.at[s], out.at[s], core)
 
     def dec_slab(tap):
         a = tap // 3
@@ -436,12 +468,20 @@
                 gp_halo_core.start()
                 gp_halo_core.wait_recv()
 
-        @pl.when(i == 1)
+        @pl.when((i == 2) & inner)
+        def _():
+            h_later.wait_recv()
+            h_halo_core.start()
+
+        @pl.when(i == 2)
         def _():
             d_core.wait_recv()
             spread(de[...].reshape(chip, chans), 0)
             d_pair.wait_recv()
             d_pair_core.start()
+
+        @pl.when(i == 4)
+        def _():
             xp_own_core.wait_recv()
             when(inner, lambda: xp_halo_core.wait_recv())
             d_pair_core.wait_recv()
@@ -455,22 +495,14 @@
         def _():
             enc_slab(tap)
 
-        @pl.when(i == 1)
-        def _():
-            @pl.when(inner)
-            def _():
-                h_later.wait_recv()
-                h_halo_core.start()
-
-        @pl.when(i == 4)
-        def _():
-            @pl.when(inner)
-            def _():
-                h_halo_core.wait_recv()
-
-            partial_conv(ys, he, wdec, (0, 1, 2), False, True)
-            total = joined(ys, False) + xe[2:4, rows].reshape(spots, chans).astype(F32)
-            output[0] = total.astype(BF16).reshape(frames, tall, wide, chans)
+    def finish_output():
+        @pl.when(inner)
+        def _():
+            h_halo_core.wait_recv()
+
+        partial_conv(ys, he, wdec, (0, 1, 2), False, True)
+        total = joined(ys, False) + xe[2:4, rows].reshape(spots, chans).astype(F32)
+        output[0] = total.astype(BF16).reshape(frames, tall, wide, chans)
 
     def s0(i):
         @pl.when(i % 2 == 0)
@@ -488,33 +520,76 @@
         total = keep[i] + r1[i].astype(F32)
         keep[i] = total
         zb[i] = total.astype(BF16)
-        for k in (2, 1, 3):
-            c_z(i, k).start()
+        when(edge, lambda: c_hand(i).start())
+        when(~edge, lambda: c_near(i).start())
 
     def s2(i):
+        @pl.when(~edge)
+        def _():
+            copy(i, 1, ra.at[i], ra.at[i], along(side_edge)).wait_recv()
+            low = jnp.where(t == 1, 16, 0)
+            at = pl.ds(pl.multiple_of(low, 16), 48)
+            keep[i, :, at] = keep[i, :, at] + ra[i].astype(F32)
+            zc[i] = keep[i, :, pl.ds(pl.multiple_of(2 * low, 16), 32)].astype(BF16)
+            c_cross(i).start()
+            c_far(i).start()
+
+    def s3(i):
         s, f1, f2, _, _ = places(i)
-        for k in (1, 2, 3):
-            c_z(i, k).wait_recv()
-        total = keep[i, :, pl.ds(pl.multiple_of(16 * t, 16), 16)]
-        for k in range(3):
-            total = total + rz[i, k].astype(F32)
+        mine = pl.ds(pl.multiple_of(16 * t, 16), 16)
+
+        @pl.when(edge)
+        def _():
+            copy(i, 1, rn.at[i], rn.at[i], along(near)).wait_recv()
+            copy(i, 3, rc.at[i], rc.at[i], along(last - near)).wait_recv()
+            keep[i, :, mine] = keep[i, :, mine] + rn[i].astype(F32)
+
+        @pl.when(~edge)
+        def _():
+            copy(i, 2, rc.at[i], rc.at[i], along(last - t)).wait_recv()
+
+        total = keep[i, :, mine] + rc[i].astype(F32)
         out[s, :, pl.ds(pl.multiple_of(128 * f1 + 64 * f2 + 16 * t, 16), 16)] = total.astype(BF16)
-        for k in (2, 1, 3):
-            c_zback(i, k).start()
-
-    def s3(i):
-        for k in (1, 2, 3):
-            c_zback(i, k).wait_recv()
-        c_secondback(i).start()
+
+        @pl.when(edge)
+        def _():
+            c_shard(i, 5, last - near).start()
+            c_shard(i, 4, near).start()
+
+        @pl.when(~edge)
+        def _():
+            c_shard(i, 6, last - t).start()
+            c_shard(i, 4, side_edge).start()
+
+    def s3b(i):
+        @pl.when(~edge)
+        def _():
+            c_arrive(i, 6, last - t).wait_recv()
+            c_arrive(i, 5, last - side_edge).wait_recv()
+            c_pass(i).start()
+            c_arrive(i, 4, side_edge).wait_recv()
+            c_own1(i).start()
+            c_own2(i).start()
+
+    def s3c(i):
+        @pl.when(edge)
+        def _():
+            c_arrive(i, 4, near).wait_recv()
+            c_arrive(i, 5, jnp.where(t == 0, 2, 0), 2).wait_recv()
+            c_own1(i).start()
+            c_own2(i).start()
 
     def s4(i):
-        c_secondback(i).wait_recv()
-        c_firstback(i).start()
-        c_coreback(i, 0).start()
+        c_own2(i).wait_recv()
+        c_on1(i).start()
+        c_own1(i).wait_recv()
+        c_on2(i).start()
 
     def s5(i):
-        c_firstback(i).wait_recv()
-        c_coreback(i, 1).start()
+        c_on1(i).wait_recv()
+        c_on2(i).wait_recv()
+        c_coreback(i).start()
+        leave(i, h, lambda c: c.start())
 
     def leave(i, hh, action):
         enc, tap = kind(i // 2, hh)
@@ -536,34 +611,44 @@
             action(to(dec_out))
 
     def s6(i):
-        c_coreback(i, 0).wait_recv()
-        c_coreback(i, 1).wait_recv()
-        leave(i, h, lambda c: c.start())
+        c_coreback(i).wait_recv()
         leave(i, 1 - h, lambda c: c.start())
 
-    stages = [s0, s1, s2, s3, s4, s5, s6]
+    stages = [s0, s1, s2, s3, s3b, s3c, s4, s5, s6]
 
     def body(i, carry):
-        for k in (6, 5, 4, 3, 2, 1, 0):
-            s = i - LAG * k
+        for k in ORDER:
+            s = i - LAGS[k]
 
             @pl.when((s >= 0) & (s < STEPS))
             def _(k=k, s=s):
                 stages[k](s)
 
+        pl.when(i == STEPS + 1)(finish_output)
         return carry
 
-    lax.fori_loop(0, STEPS + LAG * (len(stages) - 1), body, 0)
+    lax.fori_loop(0, STEPS + max(LAGS), body, 0)
 
     def finish(i, carry):
         c_second(i).wait_send()
-        for k in (1, 2, 3):
-            c_z(i, k).wait_send()
-            c_zback(i, k).wait_send()
-        c_secondback(i).wait_send()
-        c_firstback(i).wait_send()
-        c_coreback(i, 0).wait_send()
-        c_coreback(i, 1).wait_send()
+
+        @pl.when(edge)
+        def _():
+            c_hand(i).wait_send()
+            c_shard(i, 5, last - near).wait_send()
+            c_shard(i, 4, near).wait_send()
+
+        @pl.when(~edge)
+        def _():
+            c_near(i).wait_send()
+            c_cross(i).wait_send()
+            c_far(i).wait_send()
+            c_shard(i, 6, last - t).wait_send()
+            c_shard(i, 4, side_edge).wait_send()
+            c_pass(i).wait_send()
+
+        for sent in (c_own1(i), c_own2(i), c_on1(i), c_on2(i), c_coreback(i)):
+            sent.wait_send()
         leave(i, h, lambda c: c.wait())
         leave(i, 1 - h, lambda c: c.wait())
         return carry
@@ -626,13 +711,16 @@
             vmem((STEPS, 3, 64, 128), bf),
             vmem((STEPS, 3, 64, 128), bf),
             vmem((STEPS, 3, 64, 128), bf),
-            vmem((STEPS, 3, 3, 16, 128), bf),
+            vmem((STEPS, 3, 32, 128), bf),
+            vmem((STEPS, 3, 48, 128), bf),
+            vmem((STEPS, 3, 16, 128), bf),
+            vmem((STEPS, 3, 16, 128), bf),
             vmem((36, 3, chans, 128), bf),
             pltpu.SemaphoreType.DMA((2,)),
             pltpu.SemaphoreType.DMA((22,)),
             pltpu.SemaphoreType.DMA((22,)),
-            pltpu.SemaphoreType.DMA((STEPS, 11)),
-            pltpu.SemaphoreType.DMA((STEPS, 11)),
+            pltpu.SemaphoreType.DMA((STEPS, 12)),
+            pltpu.SemaphoreType.DMA((STEPS, 12)),
             pltpu.SemaphoreType.DMA((STEPS, 2)),
         ],
         compiler_params=pltpu.CompilerParams(

time: 99.5 us -> 93.2 us (0.937)
  Pallas kernels: 87.5 us -> 81.2 us
    pallas_call x1, Pallas kernels: 87.5 us -> 81.2 us  [whole_step(): pl.pallas_call(step_kernel, out_shape=[jax.ShapeDtypeStruct(video.shape,...]
where the time goes in v2:
time: 93.2 us; the launch traced here: 93 us
  Pallas kernels  81.2 us (87%)
  other arithmetic  9.83 us (11%)
  between operations  1.3 us (1%)
    pallas_call x1, Pallas kernels, whole_step(): pl.pallas_call(step_kernel, out_shape=[jax.ShapeDtypeStruct(video.shape,...  81.2 us
    reshape x2, other arithmetic, whole_step(): g.astype(F32).reshape(enc_weight.shape)  9.83 us

profile of v2, /device:TPU:1, one launch (start us, length us, event | category | flops | bytes accessed | tf_op | source)
XLA Modules:
  0.0 93.0 jit_solution(3158167034913121071)
XLA Ops:
  1.3 81.2 %shard_map.76 = (bf16[1,2,4,64,256]{4,3,2,1,0:T(8,128)(2,1)}, bf16[27,256,256]{2,1,0:T(8,128)(2,1)}, bf16[27,256,256]{2,1,0:T(8,128)(2,1)}) custom-call(s32[1]{0:T(128)S(6)} %copy.9.lengths, bf16[1,2,4,64,256]{4,3,2,1,0:T(8,128)(2,1)} %video.1, bf16[1,2,4,64,256]{4,3,2,1,0:T(8,128)(2,1)} %cot.1, bf16[27,256,256]{2,1,0:T(8,128)(2,1)} %bitcast.6, ...), custom_call_target="tpu_custom_call" | custom-call | tf_op jit(solution)/shard_map/pallas_call | solution.py:678
  82.5 0.0 copy-start
  82.5 6.0 %convert.2 = f32[3,3,3,256,256]{4,3,2,1,0:T(8,128)} convert(bf16[3,3,3,256,256]{4,3,2,1,0:T(8,128)(2,1)} %bitcast.9) | non-fusion elementwise | flops 1769472 | bytes 10616832 | tf_op jit(solution)/shard_map/reshape | solution.py:730
  88.5 0.0 copy-done
  88.5 0.0 copy-start.1
  88.5 3.8 %convert.3 = f32[3,3,3,256,256]{4,3,2,1,0:T(8,128)} convert(bf16[3,3,3,256,256]{4,3,2,1,0:T(8,128)(2,1)S(1)} %bitcast.8) | non-fusion elementwise | flops 1769472 | bytes 10616832 | tf_op jit(solution)/shard_map/reshape | solution.py:730
  92.3 0.0 copy-done.1
  92.3 0.7 copy.10
Async XLA Ops:
  82.5 6.0 %copy-start = (bf16[27,256,256]{2,1,0:T(8,128)(2,1)S(1)}, bf16[27,256,256]{2,1,0:T(8,128)(2,1)}, u32[]{:S(2)}) copy-start(bf16[27,256,256]{2,1,0:T(8,128)(2,1)} %get-tuple-element.8) | copy-start | bytes 10616836
  88.5 3.8 %copy-start.1 = (bf16[1,2,4,64,256]{4,3,2,1,0:T(8,128)(2,1)S(1)}, bf16[1,2,4,64,256]{4,3,2,1,0:T(8,128)(2,1)}, u32[]{:S(2)}) copy-start(bf16[1,2,4,64,256]{4,3,2,1,0:T(8,128)(2,1)} %get-tuple-element.12) | copy-start | bytes 786436

commit v3 on v2

--- a/solution.py
+++ b/solution.py
@@ -354,7 +354,7 @@
         return pltpu.make_async_remote_copy(
             src_ref=src,
             dst_ref=dst,
-            send_sem=ssem.at[i, slot],
+            send_sem=ssem.at[slot],
             recv_sem=rsem.at[i, slot],
             device_id=target,
             device_id_type=MESH,
@@ -629,31 +629,39 @@
 
     lax.fori_loop(0, STEPS + max(LAGS), body, 0)
 
-    def finish(i, carry):
-        c_second(i).wait_send()
-
-        @pl.when(edge)
-        def _():
-            c_hand(i).wait_send()
-            c_shard(i, 5, last - near).wait_send()
-            c_shard(i, 4, near).wait_send()
-
-        @pl.when(~edge)
-        def _():
-            c_near(i).wait_send()
-            c_cross(i).wait_send()
-            c_far(i).wait_send()
-            c_shard(i, 6, last - t).wait_send()
-            c_shard(i, 4, side_edge).wait_send()
-            c_pass(i).wait_send()
-
-        for sent in (c_own1(i), c_own2(i), c_on1(i), c_on2(i), c_coreback(i)):
-            sent.wait_send()
+    def sent_all(slot, ref):
+        copy(0, slot, ref, ref, core).wait_send()
+
+    halves = out.at[pl.ds(0, STEPS)]
+    sent_all(0, give)
+    sent_all(7, give)
+    sent_all(8, give)
+    sent_all(9, zc)
+    sent_all(10, zc)
+    sent_all(11, halves)
+
+    @pl.when(edge)
+    def _():
+        sent_all(1, ra)
+        sent_all(4, rn)
+        sent_all(5, rn)
+
+    @pl.when(~edge)
+    def _():
+        sent_all(1, rn)
+        sent_all(2, rn)
+        sent_all(3, rn)
+        sent_all(4, rn)
+        sent_all(5, zc)
+        sent_all(6, rn)
+
+
+    def left(i, carry):
         leave(i, h, lambda c: c.wait())
         leave(i, 1 - h, lambda c: c.wait())
         return carry
 
-    lax.fori_loop(0, STEPS, finish, 0)
+    lax.fori_loop(0, STEPS, left, 0)
     for sent in (x_core, g_core, xp_own, xp_own_core, gp_own, gp_own_core, d_core, d_pair, d_pair_core,
                  h_core, h_pair, h_pair_core):
         sent.wait_send()
@@ -667,6 +675,15 @@
     def _():
         for sent in (x_later, h_later, g_halo_core, gp_halo_core):
             sent.wait_send()
+
+
+def widen_kernel(output, enc_sum, dec_sum, output_out, enc_out, dec_out):
+    @pl.when(pl.program_id(0) == 0)
+    def _():
+        output_out[...] = output[...]
+
+    enc_out[...] = enc_sum[...].astype(F32)
+    dec_out[...] = dec_sum[...].astype(F32)
 
 
 def whole_step(video, lengths, enc_weight, dec_weight, cotangent):
@@ -719,7 +736,7 @@
             pltpu.SemaphoreType.DMA((2,)),
             pltpu.SemaphoreType.DMA((22,)),
             pltpu.SemaphoreType.DMA((22,)),
-            pltpu.SemaphoreType.DMA((STEPS, 12)),
+            pltpu.SemaphoreType.DMA((12,)),
             pltpu.SemaphoreType.DMA((STEPS, 12)),
             pltpu.SemaphoreType.DMA((STEPS, 2)),
         ],
@@ -727,8 +744,17 @@
             collective_id=0, has_side_effects=True, vmem_limit_bytes=56 * 2**20
         ),
     )(lengths, video, cotangent, enc27, dec27)
-    enc_grad, dec_grad = (g.astype(F32).reshape(enc_weight.shape) for g in (enc_grad, dec_grad))
-    return output, enc_grad, dec_grad
+    taps = pl.BlockSpec((9, chans, chans), lambda i: (i, 0, 0))
+    whole = pl.BlockSpec(video.shape, lambda i: (0,) * 5)
+    output, enc_grad, dec_grad = pl.pallas_call(
+        widen_kernel,
+        grid=(3,),
+        in_specs=[whole, taps, taps],
+        out_specs=[whole, taps, taps],
+        out_shape=[jax.ShapeDtypeStruct(video.shape, bf)] + [jax.ShapeDtypeStruct(enc27.shape, F32)] * 2,
+        compiler_params=pltpu.CompilerParams(vmem_limit_bytes=56 * 2**20),
+    )(output, enc_grad, dec_grad)
+    return output, enc_grad.reshape(enc_weight.shape), dec_grad.reshape(dec_weight.shape)
 
 
 def shards(video, lengths, enc_weight, dec_weight, cotangent):

time: 93.2 us -> 88.8 us (0.953)
  other arithmetic: 9.83 us -> 0 us
  Pallas kernels: 81.2 us -> 87.3 us
    reshape x2 -> x0, other arithmetic: 9.83 us -> none  [whole_step(): g.astype(F32).reshape(enc_weight.shape)]
    pallas_call x0 -> x1, Pallas kernels: none -> 7.9 us  [whole_step(): pl.pallas_call(widen_kernel, grid=(3,), in_specs=[whole, taps, taps], out...]
    pallas_call x1, Pallas kernels: 81.2 us -> 79.4 us  [whole_step(): pl.pallas_call(step_kernel, out_shape=[jax.ShapeDtypeStruct(video.shape,...]
where the time goes in v3:
time: 88.8 us; the launch traced here: 88.6 us
  Pallas kernels  87.3 us (98%)
  between operations  1.28 us (1%)
    pallas_call x1, Pallas kernels, whole_step(): pl.pallas_call(step_kernel, out_shape=[jax.ShapeDtypeStruct(video.shape,...  79.4 us
    pallas_call x1, Pallas kernels, whole_step(): pl.pallas_call(widen_kernel, grid=(3,), in_specs=[whole, taps, taps], out...  7.9 us

profile of v3, /device:TPU:1, one launch (start us, length us, event | category | flops | bytes accessed | tf_op | source)
XLA Modules:
  0.0 88.6 jit_solution(15330751995519188668)
XLA Ops:
  1.3 79.4 %shard_map.76 = (bf16[1,2,4,64,256]{4,3,2,1,0:T(8,128)(2,1)}, bf16[27,256,256]{2,1,0:T(8,128)(2,1)}, bf16[27,256,256]{2,1,0:T(8,128)(2,1)}) custom-call(s32[1]{0:T(128)S(6)} %copy.8.lengths, bf16[1,2,4,64,256]{4,3,2,1,0:T(8,128)(2,1)} %video.1, bf16[1,2,4,64,256]{4,3,2,1,0:T(8,128)(2,1)} %cot.1, bf16[27,256,256]{2,1,0:T(8,128)(2,1)} %bitcast.4, ...), custom_call_target="tpu_custom_call" | custom-call | tf_op jit(solution)/shard_map/pallas_call | solution.py:695
  80.7 7.9 %shard_map.77 = (bf16[1,2,4,64,256]{4,3,2,1,0:T(8,128)(2,1)}, f32[27,256,256]{2,1,0:T(8,128)}, f32[27,256,256]{2,1,0:T(8,128)}) custom-call(bf16[1,2,4,64,256]{4,3,2,1,0:T(8,128)(2,1)} %get-tuple-element.9.output, bf16[27,256,256]{2,1,0:T(8,128)(2,1)} %get-tuple-element.10.enc_sum, bf16[27,256,256]{2,1,0:T(8,128)(2,1)} %get-tuple-element.11.dec_sum), custom_call_target="tpu_custom_call" | custom-call | tf_op jit(solution)/shard_map/pallas_call | solution.py:749

commit v4 on v3

--- a/solution.py
+++ b/solution.py
@@ -6,6 +6,7 @@
 from jax.sharding import PartitionSpec as P
 
 MESH = pl.DeviceIdType.MESH
+WIDE = 9
 ORDER = (8, 7, 6, 5, 4, 3, 2, 1, 0)
 LAGS = (0, 5, 8, 12, 15, 17, 21, 25, 28)
 
@@ -139,9 +140,9 @@
 
 
 def step_kernel(
-    lengths, video, cot, enc_hbm, dec_hbm, output, enc_out, dec_out,
+    lengths, video, cot, enc_hbm, dec_hbm, output, out,
     wenc, wdec, xe, ge, he, de, xp, gp, hp, dp, ht, ds, ys, yg, slope,
-    yb, keep, give, r1, zb, zc, ra, rn, rc, out, wsem, hs, hr, ssem, rsem, lsem,
+    yb, keep, give, r1, zb, zc, ra, rn, rc, wsem, hs, hr, ssem, rsem,
 ):
     d, t, h = lax.axis_index("dp"), lax.axis_index("tm"), lax.axis_index("height")
     frames, tall, wide, chans = video.shape[1:]
@@ -589,30 +590,9 @@
         c_on1(i).wait_recv()
         c_on2(i).wait_recv()
         c_coreback(i).start()
-        leave(i, h, lambda c: c.start())
-
-    def leave(i, hh, action):
-        enc, tap = kind(i // 2, hh)
-        side = i % 2
-        s = 18 * enc + 2 * tap + side
-        slot = jnp.where(hh == h, 0, 1)
-
-        def to(dst):
-            return pltpu.make_async_copy(
-                out.at[s], dst.at[pl.ds(3 * tap, 3), :, pl.ds(pl.multiple_of(128 * side, 128), 128)], lsem.at[i, slot]
-            )
-
-        @pl.when(enc == 1)
-        def _():
-            action(to(enc_out))
-
-        @pl.when(enc == 0)
-        def _():
-            action(to(dec_out))
 
     def s6(i):
         c_coreback(i).wait_recv()
-        leave(i, 1 - h, lambda c: c.start())
 
     stages = [s0, s1, s2, s3, s3b, s3c, s4, s5, s6]
 
@@ -656,12 +636,6 @@
         sent_all(6, rn)
 
 
-    def left(i, carry):
-        leave(i, h, lambda c: c.wait())
-        leave(i, 1 - h, lambda c: c.wait())
-        return carry
-
-    lax.fori_loop(0, STEPS, left, 0)
     for sent in (x_core, g_core, xp_own, xp_own_core, gp_own, gp_own_core, d_core, d_pair, d_pair_core,
                  h_core, h_pair, h_pair_core):
         sent.wait_send()
@@ -677,13 +651,19 @@
             sent.wait_send()
 
 
-def widen_kernel(output, enc_sum, dec_sum, output_out, enc_out, dec_out):
-    @pl.when(pl.program_id(0) == 0)
+def widen_kernel(output, sums, output_out, enc_out, dec_out):
+    step = pl.program_id(0)
+
+    @pl.when(step == 0)
     def _():
         output_out[...] = output[...]
 
-    enc_out[...] = enc_sum[...].astype(F32)
-    dec_out[...] = dec_sum[...].astype(F32)
+    taps = enc_out.shape[0] // 3
+    for ref, first in ((dec_out, 0), (enc_out, STEPS)):
+        for k in range(taps):
+            for side in range(2):
+                part = sums[first + 2 * (taps * step + k) + side]
+                ref[3 * k : 3 * k + 3, :, 128 * side : 128 * (side + 1)] = part.astype(F32)
 
 
 def whole_step(video, lengths, enc_weight, dec_weight, cotangent):
@@ -692,12 +672,11 @@
     spots = frames * tall * wide
     ext = (4, 10, wide, chans)
     enc27, dec27 = (w.reshape(27, chans, chans) for w in (enc_weight, dec_weight))
-    output, enc_grad, dec_grad = pl.pallas_call(
+    output, sums = pl.pallas_call(
         step_kernel,
         out_shape=[
             jax.ShapeDtypeStruct(video.shape, bf),
-            jax.ShapeDtypeStruct((27, chans, chans), bf),
-            jax.ShapeDtypeStruct((27, chans, chans), bf),
+            vmem((2 * STEPS, 3, chans, 128), bf),
         ],
         in_specs=[
             pl.BlockSpec(memory_space=pltpu.SMEM),
@@ -706,7 +685,7 @@
             pl.BlockSpec(memory_space=pl.ANY),
             pl.BlockSpec(memory_space=pl.ANY),
         ],
-        out_specs=[pl.BlockSpec(memory_space=vmem)] + [pl.BlockSpec(memory_space=pl.ANY)] * 2,
+        out_specs=[pl.BlockSpec(memory_space=vmem)] * 2,
         scratch_shapes=[
             vmem((27, chans, chans), bf),
             vmem((27, chans, chans), bf),
@@ -732,28 +711,26 @@
             vmem((STEPS, 3, 48, 128), bf),
             vmem((STEPS, 3, 16, 128), bf),
             vmem((STEPS, 3, 16, 128), bf),
-            vmem((36, 3, chans, 128), bf),
             pltpu.SemaphoreType.DMA((2,)),
             pltpu.SemaphoreType.DMA((22,)),
             pltpu.SemaphoreType.DMA((22,)),
             pltpu.SemaphoreType.DMA((12,)),
             pltpu.SemaphoreType.DMA((STEPS, 12)),
-            pltpu.SemaphoreType.DMA((STEPS, 2)),
         ],
         compiler_params=pltpu.CompilerParams(
-            collective_id=0, has_side_effects=True, vmem_limit_bytes=56 * 2**20
+            collective_id=0, has_side_effects=True, vmem_limit_bytes=48 * 2**20
         ),
     )(lengths, video, cotangent, enc27, dec27)
-    taps = pl.BlockSpec((9, chans, chans), lambda i: (i, 0, 0))
+    taps = pl.BlockSpec((WIDE, chans, chans), lambda i: (i, 0, 0))
     whole = pl.BlockSpec(video.shape, lambda i: (0,) * 5)
     output, enc_grad, dec_grad = pl.pallas_call(
         widen_kernel,
-        grid=(3,),
-        in_specs=[whole, taps, taps],
+        grid=(27 // WIDE,),
+        in_specs=[whole, pl.BlockSpec(memory_space=vmem)],
         out_specs=[whole, taps, taps],
         out_shape=[jax.ShapeDtypeStruct(video.shape, bf)] + [jax.ShapeDtypeStruct(enc27.shape, F32)] * 2,
-        compiler_params=pltpu.CompilerParams(vmem_limit_bytes=56 * 2**20),
-    )(output, enc_grad, dec_grad)
+        compiler_params=pltpu.CompilerParams(vmem_limit_bytes=40 * 2**20),
+    )(output, sums)
     return output, enc_grad.reshape(enc_weight.shape), dec_grad.reshape(dec_weight.shape)
 
 

time: 88.8 us -> 86.2 us (0.971)
  Pallas kernels: 87.3 us -> 83.7 us
  local copies, waits for them, and re-layouts: 0 us -> 0.94 us
    pallas_call x1, Pallas kernels: 7.9 us -> 5.4 us  [whole_step(): pl.pallas_call(widen_kernel, grid=(27 // WIDE,), in_specs=[whole, pl.Bloc...]
    pallas_call x1, Pallas kernels: 79.4 us -> 78.3 us  [whole_step(): pl.pallas_call(step_kernel, out_shape=[jax.ShapeDtypeStruct(video.shape,...]
    unnamed x0 -> x2, local copies, waits for them, and re-layouts: none -> 0.94 us
where the time goes in v4:
time: 86.2 us; the launch traced here: 85.9 us
  Pallas kernels  83.7 us (97%)
  between operations  1.29 us (1%)
  local copies, waits for them, and re-layouts  0.94 us (1%)
    pallas_call x1, Pallas kernels, whole_step(): pl.pallas_call(step_kernel, out_shape=[jax.ShapeDtypeStruct(video.shape,...  78.3 us
    pallas_call x1, Pallas kernels, whole_step(): pl.pallas_call(widen_kernel, grid=(27 // WIDE,), in_specs=[whole, pl.Bloc...  5.4 us

profile of v4, /device:TPU:1, one launch (start us, length us, event | category | flops | bytes accessed | tf_op | source)
XLA Modules:
  0.0 85.9 jit_solution(5737744518957414165)
XLA Ops:
  1.3 78.3 %shard_map.76 = (bf16[1,2,4,64,256]{4,3,2,1,0:T(8,128)(2,1)}, bf16[36,3,256,128]{3,2,1,0:T(8,128)(2,1)S(1)}) custom-call(s32[1]{0:T(128)S(6)} %copy.8.lengths, bf16[1,2,4,64,256]{4,3,2,1,0:T(8,128)(2,1)} %video.1, bf16[1,2,4,64,256]{4,3,2,1,0:T(8,128)(2,1)} %cot.1, bf16[27,256,256]{2,1,0:T(8,128)(2,1)} %bitcast.4, bf16[27,256,256]{2,1,0:T(8,128)(2,1)} %bitcast.5), custom_call_target="tpu_custom_call" | custom-call | tf_op jit(solution)/shard_map/pallas_call | solution.py:675
  79.6 0.0 copy-start
  79.6 0.9 %copy-done = bf16[1,2,4,64,256]{4,3,2,1,0:T(8,128)(2,1)S(1)} copy-done((bf16[1,2,4,64,256]{4,3,2,1,0:T(8,128)(2,1)S(1)}, bf16[1,2,4,64,256]{4,3,2,1,0:T(8,128)(2,1)}, u32[]{:S(2)}) %copy-start) | copy-done | bytes 262168
  80.5 5.4 %shard_map.77 = (bf16[1,2,4,64,256]{4,3,2,1,0:T(8,128)(2,1)}, f32[27,256,256]{2,1,0:T(8,128)}, f32[27,256,256]{2,1,0:T(8,128)}) custom-call(bf16[1,2,4,64,256]{4,3,2,1,0:T(8,128)(2,1)S(1)} %copy-done, bf16[36,3,256,128]{3,2,1,0:T(8,128)(2,1)S(1)} %get-tuple-element.9.sums), custom_call_target="tpu_custom_call" | custom-call | tf_op jit(solution)/shard_map/pallas_call | solution.py:726
Async XLA Ops:
  79.6 1.0 %copy-start = (bf16[1,2,4,64,256]{4,3,2,1,0:T(8,128)(2,1)S(1)}, bf16[1,2,4,64,256]{4,3,2,1,0:T(8,128)(2,1)}, u32[]{:S(2)}) copy-start(bf16[1,2,4,64,256]{4,3,2,1,0:T(8,128)(2,1)} %get-tuple-element.8.output) | copy-start | bytes 786436

commit v5 on v4

--- a/solution.py
+++ b/solution.py
@@ -8,7 +8,7 @@
 MESH = pl.DeviceIdType.MESH
 WIDE = 9
 ORDER = (8, 7, 6, 5, 4, 3, 2, 1, 0)
-LAGS = (0, 5, 8, 12, 15, 17, 21, 25, 28)
+LAGS = (0, 5, 8, 12, 15, 18, 22, 26, 29)
 
 
 def extended(shard, sides, width):

time: 86.2 us -> 85.4 us (level)
  no operation moved by 1% of the time
where the time goes in v5:
time: 85.4 us; the launch traced here: 85.1 us
  Pallas kernels  82.9 us (97%)
  between operations  1.29 us (2%)
  local copies, waits for them, and re-layouts  0.94 us (1%)
    pallas_call x1, Pallas kernels, whole_step(): pl.pallas_call(step_kernel, out_shape=[jax.ShapeDtypeStruct(video.shape,...  77.5 us
    pallas_call x1, Pallas kernels, whole_step(): pl.pallas_call(widen_kernel, grid=(27 // WIDE,), in_specs=[whole, pl.Bloc...  5.4 us

profile of v5, /device:TPU:1, one launch (start us, length us, event | category | flops | bytes accessed | tf_op | source)
XLA Modules:
  0.0 85.1 jit_solution(14025363174341851602)
XLA Ops:
  1.3 77.5 %shard_map.76 = (bf16[1,2,4,64,256]{4,3,2,1,0:T(8,128)(2,1)}, bf16[36,3,256,128]{3,2,1,0:T(8,128)(2,1)S(1)}) custom-call(s32[1]{0:T(128)S(6)} %copy.8.lengths, bf16[1,2,4,64,256]{4,3,2,1,0:T(8,128)(2,1)} %video.1, bf16[1,2,4,64,256]{4,3,2,1,0:T(8,128)(2,1)} %cot.1, bf16[27,256,256]{2,1,0:T(8,128)(2,1)} %bitcast.4, bf16[27,256,256]{2,1,0:T(8,128)(2,1)} %bitcast.5), custom_call_target="tpu_custom_call" | custom-call | tf_op jit(solution)/shard_map/pallas_call | solution.py:675
  78.8 0.0 copy-start
  78.8 0.9 %copy-done = bf16[1,2,4,64,256]{4,3,2,1,0:T(8,128)(2,1)S(1)} copy-done((bf16[1,2,4,64,256]{4,3,2,1,0:T(8,128)(2,1)S(1)}, bf16[1,2,4,64,256]{4,3,2,1,0:T(8,128)(2,1)}, u32[]{:S(2)}) %copy-start) | copy-done | bytes 262168
  79.7 5.4 %shard_map.77 = (bf16[1,2,4,64,256]{4,3,2,1,0:T(8,128)(2,1)}, f32[27,256,256]{2,1,0:T(8,128)}, f32[27,256,256]{2,1,0:T(8,128)}) custom-call(bf16[1,2,4,64,256]{4,3,2,1,0:T(8,128)(2,1)S(1)} %copy-done, bf16[36,3,256,128]{3,2,1,0:T(8,128)(2,1)S(1)} %get-tuple-element.9.sums), custom_call_target="tpu_custom_call" | custom-call | tf_op jit(solution)/shard_map/pallas_call | solution.py:726
Async XLA Ops:
  78.8 1.0 %copy-start = (bf16[1,2,4,64,256]{4,3,2,1,0:T(8,128)(2,1)S(1)}, bf16[1,2,4,64,256]{4,3,2,1,0:T(8,128)(2,1)}, u32[]{:S(2)}) copy-start(bf16[1,2,4,64,256]{4,3,2,1,0:T(8,128)(2,1)} %get-tuple-element.8.output) | copy-start | bytes 786436

commit v6 on v5

--- a/solution.py
+++ b/solution.py
@@ -162,9 +162,14 @@
     w_dec.start()
 
     barrier = pltpu.get_barrier_semaphore()
-    partners = [core, xdev, ydev] + [(d, lax.rem(t + k, last + 1), h) for k in range(1, 4)]
-    for partner in partners:
+
+    def greet(partner):
         pl.semaphore_signal(barrier, inc=1, device_id=partner, device_id_type=MESH)
+
+    for k in (-2, -1, 1, 2):
+        pl.when((t + k >= 0) & (t + k <= last))(lambda k=k: greet((d, t + k, h)))
+    for partner in (core, xdev, ydev):
+        greet(partner)
 
     rows = pl.ds(1 + base, tall)
     own_rows = pl.ds(base, tall)
@@ -176,7 +181,7 @@
         live = t * frames + f < lengths[0]
         xe[2 + f, rows] = jnp.where(live, video[0, f], jnp.zeros_like(video[0, f]))
         ge[f, rows] = jnp.where(live, cot[0, f], jnp.zeros_like(cot[0, f]))
-    pl.semaphore_wait(barrier, len(partners))
+    pl.semaphore_wait(barrier, jnp.where((t == 0) | (t == last), 5, 6))
 
     def message(slot, src, dst, target):
         return pltpu.make_async_remote_copy(
@@ -356,7 +361,7 @@
             src_ref=src,
             dst_ref=dst,
             send_sem=ssem.at[slot],
-            recv_sem=rsem.at[i, slot],
+            recv_sem=rsem.at[i, slot - (slot > 2)],
             device_id=target,
             device_id_type=MESH,
         )
@@ -715,7 +720,7 @@
             pltpu.SemaphoreType.DMA((22,)),
             pltpu.SemaphoreType.DMA((22,)),
             pltpu.SemaphoreType.DMA((12,)),
-            pltpu.SemaphoreType.DMA((STEPS, 12)),
+            pltpu.SemaphoreType.DMA((STEPS, 11)),
         ],
         compiler_params=pltpu.CompilerParams(
             collective_id=0, has_side_effects=True, vmem_limit_bytes=48 * 2**20

time: 85.4 us -> 85.3 us (level)
  no operation moved by 1% of the time
where the time goes in v6:
time: 85.3 us; the launch traced here: 85 us
  Pallas kernels  82.8 us (97%)
  between operations  1.29 us (2%)
  local copies, waits for them, and re-layouts  0.94 us (1%)
    pallas_call x1, Pallas kernels, whole_step(): pl.pallas_call(step_kernel, out_shape=[jax.ShapeDtypeStruct(video.shape,...  77.4 us
    pallas_call x1, Pallas kernels, whole_step(): pl.pallas_call(widen_kernel, grid=(27 // WIDE,), in_specs=[whole, pl.Bloc...  5.4 us

profile of v6, /device:TPU:1, one launch (start us, length us, event | category | flops | bytes accessed | tf_op | source)
XLA Modules:
  0.0 85.0 jit_solution(17267716023109770570)
XLA Ops:
  1.3 77.4 %shard_map.76 = (bf16[1,2,4,64,256]{4,3,2,1,0:T(8,128)(2,1)}, bf16[36,3,256,128]{3,2,1,0:T(8,128)(2,1)S(1)}) custom-call(s32[1]{0:T(128)S(6)} %copy.8.lengths, bf16[1,2,4,64,256]{4,3,2,1,0:T(8,128)(2,1)} %video.1, bf16[1,2,4,64,256]{4,3,2,1,0:T(8,128)(2,1)} %cot.1, bf16[27,256,256]{2,1,0:T(8,128)(2,1)} %bitcast.4, bf16[27,256,256]{2,1,0:T(8,128)(2,1)} %bitcast.5), custom_call_target="tpu_custom_call" | custom-call | tf_op jit(solution)/shard_map/pallas_call | solution.py:680
  78.7 0.0 copy-start
  78.7 0.9 %copy-done = bf16[1,2,4,64,256]{4,3,2,1,0:T(8,128)(2,1)S(1)} copy-done((bf16[1,2,4,64,256]{4,3,2,1,0:T(8,128)(2,1)S(1)}, bf16[1,2,4,64,256]{4,3,2,1,0:T(8,128)(2,1)}, u32[]{:S(2)}) %copy-start) | copy-done | bytes 262168
  79.6 5.4 %shard_map.77 = (bf16[1,2,4,64,256]{4,3,2,1,0:T(8,128)(2,1)}, f32[27,256,256]{2,1,0:T(8,128)}, f32[27,256,256]{2,1,0:T(8,128)}) custom-call(bf16[1,2,4,64,256]{4,3,2,1,0:T(8,128)(2,1)S(1)} %copy-done, bf16[36,3,256,128]{3,2,1,0:T(8,128)(2,1)S(1)} %get-tuple-element.9.sums), custom_call_target="tpu_custom_call" | custom-call | tf_op jit(solution)/shard_map/pallas_call | solution.py:731
Async XLA Ops:
  78.7 1.0 %copy-start = (bf16[1,2,4,64,256]{4,3,2,1,0:T(8,128)(2,1)S(1)}, bf16[1,2,4,64,256]{4,3,2,1,0:T(8,128)(2,1)}, u32[]{:S(2)}) copy-start(bf16[1,2,4,64,256]{4,3,2,1,0:T(8,128)(2,1)} %get-tuple-element.8.output) | copy-start | bytes 786436
